TPU v7x, 32 devices: a whole 2x2x4 slice. The times are simulated.
32 devices in a mesh: layer: 4 (over y, x), phi: 8 (over z, core).
Axes of the slice: x: 2, y: 2, z: 4, core: 2. Of those that a mesh axis runs over, the one named last changes fastest.
Arguments:
- hits: bfloat16 [4, 8, 8192, 128], P('layer', 'phi'), may hold values from -6 to 6
- attach_index: int32 [4, 8, 4, 8192], P('layer', 'phi'), may hold values from 0 to 1023, as said below
- attach_weight: bfloat16 [4, 8, 4, 8192], P('layer', 'phi'), may hold values from 0.049804688 to 1
- shard_counts: int32 [4, 8], P('layer', 'phi'), may hold values from 1024 to 8192, as said below
- edge_source: int32 [8, 8, 1024], P('phi'), may hold values from 0 to 2047
- cotangent: bfloat16 [8, 1024, 128], P('phi'), may hold values from -12 to 12
- w_message: bfloat16 [128, 128], replicated, may hold values from -0.5 to 0.5
- w_edge: bfloat16 [128, 128], replicated, may hold values from -0.5 to 0.5
- w_output: bfloat16 [128, 128], replicated, may hold values from -0.5 to 0.5
Outputs:
- d_hits: bfloat16 [4, 8, 8192, 128], P('layer', 'phi')
- grad_message: float32 [128, 128], replicated
- grad_edge: float32 [128, 128], replicated
- grad_output: float32 [128, 128], replicated
Inputs may be any that keep to these rules, and one draw needn't show every extreme that they name: `attach_index`: A hit's four super-nodes are different. `shard_counts`: slots from the count on are padding; at least one shard is full. `edge_source`: row r of a sector's extended list is the previous sector's super-node 1024 - 512 + r for r < 512, its own super-node r - 512 below 1536, and else the next sector's super-node r - 1536.
All inputs are finite; a program needn't handle non-finite values.
Results may differ from a plain program's by a relative error of at most 0.015.
Values may be sent and summed in bfloat16 or wider, within the bound.
A program may use at most 64 MiB of HBM per device.

v0:
```python
import math

import jax
import jax.numpy as jnp
from jax import lax
from jax.sharding import PartitionSpec as P


def with_halo(cells, sides, width):
    for axis, dim in sides:
        count = lax.axis_size(axis)
        head = lax.slice_in_dim(cells, 0, width, axis=dim)
        tail = lax.slice_in_dim(cells, cells.shape[dim] - width, cells.shape[dim], axis=dim)
        cells = jnp.concatenate(
            [
                lax.ppermute(tail, axis, [(i, (i + 1) % count) for i in range(count)]),
                cells,
                lax.ppermute(head, axis, [((i + 1) % count, i) for i in range(count)]),
            ],
            axis=dim,
        )
    return cells


def one_hot_tile(node_iota, index_blk, weight_blk):
    zero_value = jnp.zeros((), jnp.bfloat16)
    tile_sum = jnp.where(node_iota == index_blk[0][None, :], weight_blk[0][None, :], zero_value)
    for slot in range(1, index_blk.shape[0]):
        tile_sum = tile_sum + jnp.where(
            node_iota == index_blk[slot][None, :], weight_blk[slot][None, :], zero_value
        )
    return tile_sum


def normalize(totals, masses):
    scale = (1.0 / jnp.sqrt(1.0 + masses)).astype(jnp.bfloat16)
    node = (totals * scale.astype(jnp.float32)[:, None]).astype(jnp.bfloat16)
    return (node, scale)


def contract_rows(left, right):
    return lax.dot_general(
        left, right, (((0,), (0,)), ((), ())), preferred_element_type=jnp.float32
    )


def shards(
    hits,
    attach_index,
    attach_weight,
    shard_counts,
    edge_source,
    cotangent,
    w_message,
    w_edge,
    w_output,
):
    hit_block = hits[0, 0]
    hit_rows = hit_block.shape[0]
    features = hit_block.shape[1]
    nodes = cotangent.shape[1]
    rim_rows = nodes // 2
    layer_count = lax.axis_size("layer")
    sector_count = lax.axis_size("phi")
    share_rows = nodes // layer_count
    block_rows = min(512, hit_rows)
    block_count = hit_rows // block_rows
    grad_cot = cotangent[0]
    sources = edge_source[0]
    positions = jnp.arange(hit_rows, dtype=jnp.int32)
    realness = (positions < shard_counts[0, 0]).astype(jnp.bfloat16)
    weight_table = attach_weight[0, 0] * realness[None, :]
    index_table = attach_index[0, 0]
    message = jnp.tanh(jnp.dot(hit_block, w_message, preferred_element_type=jnp.float32)).astype(
        jnp.bfloat16
    )
    node_iota = jnp.arange(nodes, dtype=jnp.int32)[:, None]
    index_blocks = jnp.transpose(index_table.reshape(4, block_count, block_rows), (1, 0, 2))
    weight_blocks = jnp.transpose(weight_table.reshape(4, block_count, block_rows), (1, 0, 2))
    message_blocks = message.reshape(block_count, block_rows, features)

    def pool_step(carry, inputs):
        totals, masses = carry
        index_blk, weight_blk, message_blk = inputs
        tile_now = one_hot_tile(node_iota, index_blk, weight_blk)
        totals = totals + jnp.dot(tile_now, message_blk, preferred_element_type=jnp.float32)
        masses = masses + jnp.sum(tile_now.astype(jnp.float32), axis=1)
        return ((totals, masses), None)

    start_carry = (jnp.zeros((nodes, features), jnp.float32), jnp.zeros((nodes,), jnp.float32))
    (pooled, masses), _ = lax.scan(
        pool_step, start_carry, (index_blocks, weight_blocks, message_blocks)
    )
    totals, mass_sum = lax.psum((pooled, masses), "layer")
    node, scale = normalize(totals, mass_sum)
    preact = jnp.dot(node, w_edge, preferred_element_type=jnp.float32)
    sigma = jax.nn.sigmoid(preact)
    edge_msg = (preact * sigma).astype(jnp.bfloat16)
    beside_all = with_halo(edge_msg[None], (("phi", 0),), 1)
    lower_rim = beside_all[0, nodes - rim_rows :]
    upper_rim = beside_all[2, :rim_rows]
    extended = jnp.concatenate([lower_rim, edge_msg, upper_rim], axis=0)
    ext_iota = jnp.arange(nodes + 2 * rim_rows, dtype=jnp.int32)[None, :, None]
    adjacency = jnp.sum((ext_iota == sources[:, None, :]).astype(jnp.float32), axis=0).astype(
        jnp.bfloat16
    )
    gathered = contract_rows(adjacency, extended).astype(jnp.bfloat16)
    d_gathered = jnp.dot(grad_cot, w_output.T, preferred_element_type=jnp.float32).astype(
        jnp.bfloat16
    )
    spread = jnp.dot(adjacency, d_gathered, preferred_element_type=jnp.float32)
    edges_back = jnp.stack([spread[:rim_rows], spread[nodes + rim_rows :]])[None]
    returned = with_halo(edges_back, (("phi", 0),), 1)
    from_upper = returned[2, 0]
    from_lower = returned[0, 1]
    d_edge = spread[rim_rows : rim_rows + nodes]
    d_edge = d_edge.at[nodes - rim_rows :].add(from_upper)
    d_edge = d_edge.at[:rim_rows].add(from_lower)
    d_pre = (d_edge * (sigma * (1.0 + preact * (1.0 - sigma)))).astype(jnp.bfloat16)
    back_node = jnp.dot(d_pre, w_edge.T, preferred_element_type=jnp.float32)
    d_node = (
        (grad_cot.astype(jnp.float32) + back_node) * scale.astype(jnp.float32)[:, None]
    ).astype(jnp.bfloat16)
    share_start = lax.axis_index("layer") * share_rows
    gathered_share = lax.dynamic_slice_in_dim(gathered, share_start, share_rows, 0)
    grad_share = lax.dynamic_slice_in_dim(grad_cot, share_start, share_rows, 0)
    node_share = lax.dynamic_slice_in_dim(node, share_start, share_rows, 0)
    d_pre_share = lax.dynamic_slice_in_dim(d_pre, share_start, share_rows, 0)
    output_term = contract_rows(gathered_share, grad_share)
    edge_term = contract_rows(node_share, d_pre_share)

    def back_step(carry, inputs):
        index_blk, weight_blk, message_blk = inputs
        tile_now = one_hot_tile(node_iota, index_blk, weight_blk)
        d_message = contract_rows(tile_now, d_node)
        message_f = message_blk.astype(jnp.float32)
        return (carry, (d_message * (1.0 - message_f * message_f)).astype(jnp.bfloat16))

    _, d_act_blocks = lax.scan(back_step, 0, (index_blocks, weight_blocks, message_blocks))
    d_act = d_act_blocks.reshape(hit_rows, features)
    d_hits = jnp.dot(d_act, w_message.T, preferred_element_type=jnp.float32).astype(jnp.bfloat16)
    message_term = contract_rows(hit_block, d_act)
    summed = lax.psum((message_term, edge_term, output_term), ("layer", "phi"))
    hit_norm = math.sqrt(layer_count * sector_count * hit_rows)
    node_norm = math.sqrt(sector_count * nodes)
    return (d_hits[None, None], summed[0] / hit_norm, summed[1] / node_norm, summed[2] / node_norm)


def solution(mesh):
    placed = (
        P("layer", "phi", None, None),
        P("layer", "phi", None, None),
        P("layer", "phi", None, None),
        P("layer", "phi"),
        P("phi", None, None),
        P("phi", None, None),
        P(),
        P(),
        P(),
    )
    return jax.shard_map(
        shards,
        mesh=mesh,
        in_specs=placed,
        out_specs=(P("layer", "phi", None, None), P(), P(), P()),
        check_vma=False,
    )
```

profile of v0, /device:TPU:0, one launch (start us, length us, event | category | flops | bytes accessed | tf_op | source)
XLA Modules:
  0.0 366.7 jit_solution(7830874262734797815)
XLA Ops:
  7.2 14.9 %convert_reduce_fusion.1 = bf16[2048,1024]{1,0:T(8,128)(2,1)} fusion(s32[8,1024]{1,0:T(8,128)} %bitcast.123), kind=kLoop, calls=%fused_computation.69 | loop fusion | flops 48234496 | bytes 4227072 | tf_op jit(solution)/shard_map/reduce_sum | solution.py:104
  22.1 3.7 %fusion.55 = f32[2048,128]{1,0:T(8,128)S(1)} fusion(bf16[2048,1024]{1,0:T(8,128)(2,1)} %convert_reduce_fusion.1, bf16[128,128]{1,0:T(8,128)(2,1)S(1)} %copy-done.5, bf16[1,1024,128]{2,1,0:T(8,128)(2,1)S(1)} %copy-done.2), kind=kOutput, calls=%fused_computation.80 | convolution fusion | flops 570556416 | bytes 5537792 | tf_op jit(solution)/shard_map/dot_general | solution.py:111
  26.7 4.5 %collective-permute-start = (f32[1,2,512,128]{3,2,1,0:T(8,128)}, f32[1,2,512,128]{3,2,1,0:T(8,128)}, u32[]{:S(2)}, u32[]{:S(2)}) collective-permute-start(f32[1,2,512,128]{3,2,1,0:T(8,128)} %maximum_bitcast_fusion), channel_id=1, source_target_pairs={{1,0},{2,1},{3,2},{4,3},{5,4},{6,5},{7,6},{0,7},{9,8},{10,9},{11,1... | collective-permute-start | bytes 1572872 | tf_op jit(solution)/shard_map/ppermute | solution.py:18
  31.9 2.0 fusion.48
  34.0 77.8 %while.29 = (s32[]{:T(128)}, f32[1024,128]{1,0:T(8,128)}, f32[1024]{0:T(1024)S(1)}, s32[16,4,512]{2,1,0:T(4,128)}, bf16[16,4,512]{2,1,0:T(4,128)(2,1)S(1)}, /*in...) while((s32[]{:T(128)}, f32[1024,128]{1,0:T(8,128)}, ...), condition=%wide.region_3.4_spmd.clone.clone, body=%wide.region_1.3_spmd.clone.clone.sunk | while | flops 151782400 | bytes 1245884 | solution.py:91
  34.9 2.8 convolution_add_fusion.3
  37.7 0.9 convert_reduce_fusion.3
  39.6 3.0 convolution_add_fusion.3
  42.6 0.9 convert_reduce_fusion.3
  44.5 3.0 convolution_add_fusion.3
  47.5 0.9 convert_reduce_fusion.3
  49.3 3.0 convolution_add_fusion.3
  54.2 3.0 convolution_add_fusion.3
  57.2 0.9 convert_reduce_fusion.3
  59.1 3.0 convolution_add_fusion.3
  62.1 0.9 convert_reduce_fusion.3
  63.9 3.0 convolution_add_fusion.3
  67.0 0.9 convert_reduce_fusion.3
  68.8 3.0 convolution_add_fusion.3
  71.8 0.9 convert_reduce_fusion.3
  73.7 3.0 convolution_add_fusion.3
  76.7 0.9 convert_reduce_fusion.3
  78.6 3.0 convolution_add_fusion.3
  81.6 0.9 convert_reduce_fusion.3
  83.4 3.0 convolution_add_fusion.3
  86.5 0.9 convert_reduce_fusion.3
  88.3 3.0 convolution_add_fusion.3
  91.3 0.9 convert_reduce_fusion.3
  93.2 3.0 convolution_add_fusion.3
  98.1 3.0 convolution_add_fusion.3
  101.1 0.9 convert_reduce_fusion.3
  102.9 3.0 convolution_add_fusion.3
  107.8 3.0 convolution_add_fusion.3
  110.8 0.9 convert_reduce_fusion.3
  111.8 10.0 %psum.36 = f32[1024]{0:T(1024)S(1)} all-reduce(f32[1024]{0:T(1024)S(1)} %get-tuple-element.122), channel_id=1, replica_groups=mesh['layer'=4,'phi'=8] {'layer'}, use_global_device_ids=true, to_apply=%region_5.6 | all-reduce | flops 1024 | bytes 8192 | tf_op jit(solution)/shard_map/psum | solution.py:94
  122.8 1.7 fusion.70
  124.5 1.8 fusion.68
  126.2 32.3 %all-reduce.4.cloned.1.call-done = f32[1024,128]{1,0:T(8,128)} async-done(((f32[1024,128]{1,0:T(8,128)}), f32[1024,128]{1,0:T(8,128)}) %all-reduce.4.cloned.1.call-update) | async-done | bytes 524304 | tf_op jit(solution)/shard_map/psum | solution.py:94
  158.5 1.2 multiply_convert_fusion.2
  159.8 2.2 multiply_convert_fusion
  161.9 2.6 collective-permute-start.3
  164.8 59.3 %while.28 = (s32[]{:T(128)}, bf16[16,512,128]{2,1,0:T(8,128)(2,1)}, s32[16,4,512]{2,1,0:T(4,128)}, bf16[16,4,512]{2,1,0:T(4,128)(2,1)S(1)}, bf16[1024,128]{1,0:T...) while((s32[]{:T(128)}, bf16[16,512,128]{2,1,0:T(8,128)(2,1)}, ...), condition=%wide.region_7.8_spmd.clone.clone, body=%wide.region_6.7_spmd.clone.clone.sunk | while | flops 142934016 | bytes 561841 | solution.py:139
  165.7 2.8 fusion.106
  169.4 2.8 fusion.106
  173.1 2.8 fusion.106
  176.8 2.8 fusion.106
  180.5 2.8 fusion.106
  184.2 2.8 fusion.106
  187.9 2.8 fusion.106
  191.6 2.8 fusion.106
  195.3 2.8 fusion.106
  199.0 2.8 fusion.106
  202.7 2.8 fusion.106
  206.4 2.8 fusion.106
  210.1 2.8 fusion.106
  213.9 2.8 fusion.106
  217.6 2.8 fusion.106
  221.3 2.8 fusion.106
  224.1 3.1 fusion.59
  228.0 0.9 slice_bitcast_fusion.4
  229.0 2.3 fusion.53
  232.1 3.6 fusion.49
  235.7 121.0 %all-reduce.6.cloned.1.call-done = (f32[128,128]{0,1:T(8,128)}, f32[128,128]{1,0:T(8,128)}, f32[128,128]{1,0:T(8,128)}) async-done(((f32[128,128]{0,1:T(8,128)}, f32[128,128]{1,0:T(8,128)}, f32[128,128]{1,0:T(8,128)}), (f32[128,128]{0,1:T(8,128)}, f32[128,128]{1,0:T(8,128)}, f32[128,128]{1,0:T(8,128)})) %all-reduce.6.cloned.1.call-update) | async-done | bytes 196624 | tf_op jit(solution)/shard_map/psum | solution.py:143
  358.3 1.5 broadcast_multiply_fusion
  (122 shorter events, 37.3 us)
Async XLA Ops:
  7.2 24.7 %copy-start = (bf16[1,1,8192,128]{3,2,1,0:T(8,128)(2,1)S(1)}, bf16[1,1,8192,128]{3,2,1,0:T(8,128)(2,1)}, u32[]{:S(2)}) copy-start(bf16[1,1,8192,128]{3,2,1,0:T(8,128)(2,1)} %param.17) | copy-start | bytes 6291460
  7.2 151.4 %all-reduce.4.cloned.1.call-start = ((), (), s32[]{:S(2)}) async-start(), calls=%async_computation | async-start | bytes 1048576 | tf_op jit(solution)/shard_map/psum | solution.py:94
  7.2 14.9 %copy-start.2 = (bf16[1,1024,128]{2,1,0:T(8,128)(2,1)S(1)}, bf16[1,1024,128]{2,1,0:T(8,128)(2,1)}, u32[]{:S(2)}) copy-start(bf16[1,1024,128]{2,1,0:T(8,128)(2,1)} %param.22) | copy-start | bytes 786436
  7.2 14.9 %copy-start.5 = (bf16[128,128]{1,0:T(8,128)(2,1)S(1)}, bf16[128,128]{1,0:T(8,128)(2,1)}, u32[]{:S(2)}) copy-start(bf16[128,128]{1,0:T(8,128)(2,1)} %param.25) | copy-start | bytes 98308
  25.8 6.1 %copy-start.3 = (bf16[128,128]{1,0:T(8,128)(2,1)S(1)}, bf16[128,128]{1,0:T(8,128)(2,1)}, u32[]{:S(2)}) copy-start(bf16[128,128]{1,0:T(8,128)(2,1)} %param.23) | copy-start | bytes 98308
  26.7 96.0 %collective-permute-start = (f32[1,2,512,128]{3,2,1,0:T(8,128)}, f32[1,2,512,128]{3,2,1,0:T(8,128)}, u32[]{:S(2)}, u32[]{:S(2)}) collective-permute-start(f32[1,2,512,128]{3,2,1,0:T(8,128)} %maximum_bitcast_fusion), channel_id=1, source_target_pairs={{1,0},{2,1},{3,2},{4,3},{5,4},{6,5},{7,6},{0,7},{9,8},{10,9},{11,1... | collective-permute-start | bytes 1572872 | tf_op jit(solution)/shard_map/ppermute | solution.py:18
  31.2 93.2 %collective-permute-start.1 = (f32[1,2,512,128]{3,2,1,0:T(8,128)}, f32[1,2,512,128]{3,2,1,0:T(8,128)}, u32[]{:S(2)}, u32[]{:S(2)}) collective-permute-start(f32[1,2,512,128]{3,2,1,0:T(8,128)} %maximum_bitcast_fusion), channel_id=1, source_target_pairs={{0,1},{1,2},{2,3},{3,4},{4,5},{5,6},{6,7},{7,0},{8,9},{9,10},{10,1... | collective-permute-start | bytes 1572872 | tf_op jit(solution)/shard_map/ppermute | solution.py:16
  31.9 2.0 copy-start.4
  111.8 48.0 %copy-start.6 = (bf16[128,128]{1,0:T(8,128)(2,1)S(1)}, bf16[128,128]{1,0:T(8,128)(2,1)}, u32[]{:S(2)}) copy-start(bf16[128,128]{1,0:T(8,128)(2,1)} %param.24) | copy-start | bytes 98308
  111.8 244.9 %all-reduce.6.cloned.1.call-start = ((), (), s32[]{:S(2)}) async-start(), calls=%async_computation.1 | async-start | bytes 393216 | tf_op jit(solution)/shard_map/psum | solution.py:143
  161.9 66.1 %collective-permute-start.3 = (bf16[1,1024,128]{2,1,0:T(8,128)(2,1)}, bf16[1,1024,128]{2,1,0:T(8,128)(2,1)}, u32[]{:S(2)}, u32[]{:S(2)}) collective-permute-start(bf16[1,1024,128]{2,1,0:T(8,128)(2,1)} %bitcast.18), channel_id=1, source_target_pairs={{1,0},{2,1},{3,2},{4,3},{5,4},{6,5},{7,6},{0,7},{9,8},{10,9},{11,1... | collective-permute-start | bytes 786440 | tf_op jit(solution)/shard_map/ppermute | solution.py:18
  164.5 64.4 %collective-permute-start.2 = (bf16[1,1024,128]{2,1,0:T(8,128)(2,1)}, bf16[1,1024,128]{2,1,0:T(8,128)(2,1)S(1)}, u32[]{:S(2)}, u32[]{:S(2)}) collective-permute-start(bf16[1,1024,128]{2,1,0:T(8,128)(2,1)} %bitcast.18), channel_id=1, source_target_pairs={{0,1},{1,2},{2,3},{3,4},{4,5},{5,6},{6,7},{7,0},{8,9},{9,10},{10,1... | collective-permute-start | bytes 786440 | tf_op jit(solution)/shard_map/ppermute | solution.py:16
  224.1 4.9 %copy-start.1 = (bf16[2048,1024]{1,0:T(8,128)(2,1)S(1)}, bf16[2048,1024]{1,0:T(8,128)(2,1)}, u32[]{:S(2)}) copy-start(bf16[2048,1024]{1,0:T(8,128)(2,1)} %convert_reduce_fusion.1) | copy-start | bytes 12582916
Sparse Core Ops, SparseCore 0:
  111.9 46.5 all-reduce.3
  232.2 124.4 all-reduce.5
where the time goes:
time: 370 us; the launch traced here: 367 us
  waiting for transfers between devices  153 us (41%)
  matrix products  112 us (30%)
  other arithmetic  37.5 us (10%)
  local copies, waits for them, and re-layouts  31.6 us (9%)
  between operations  14.8 us (4%)
  blocking collectives  10 us (3%)
  starting transfers between devices  7.16 us (2%)
    psum x1, waiting for transfers between devices, shards(): summed = lax.psum((message_term, edge_term, output_term), ('layer', 'phi'))  121 us
    dot_general x20, matrix products, contract_rows(): lax.dot_general(left, right, (((0,), (0,)), ((), ())), preferred_element_...  51.8 us
    dot_general x16, matrix products, pool_step(): jnp.dot(tile_now, message_blk, preferred_element_type=jnp.float32)  48 us
    psum x1, waiting for transfers between devices, shards(): totals, mass_sum = lax.psum((pooled, masses), 'layer')  32.3 us
    slice x32, local copies, waits for them, and re-layouts, one_hot_tile(): index_blk[0][None, :]  27.4 us
    reduce_sum x1, other arithmetic, shards(): jnp.sum((ext_iota == sources[:, None, :]).astype(jnp.float32), axis=0)  14.9 us
    reduce_sum x16, other arithmetic, pool_step(): masses = masses + jnp.sum(tile_now.astype(jnp.float32), axis=1)  14.5 us
    psum x1, blocking collectives, shards(): totals, mass_sum = lax.psum((pooled, masses), 'layer')  10 us
  transfers between devices with their start and end apart: 6, of which 2 were waited for; matrix products, arithmetic and copies ran while one was open for 41% of the time, Pallas kernels for 0%

commit v1 on v0

v1 whole, which is shorter than its diff:
```python
import functools
import math

import jax
import jax.numpy as jnp
from jax import lax
from jax.experimental import pallas as pl
from jax.experimental.pallas import tpu as pltpu
from jax.sharding import PartitionSpec as P

BF = jnp.bfloat16
F32 = jnp.float32
LANES = 128
PACK = 16


def dot(a, b):
    return jnp.dot(a, b, preferred_element_type=F32)


def dot_nt(a, b):
    return lax.dot_general(a, b, (((1,), (1,)), ((), ())), preferred_element_type=F32)


def dot_tn(a, b):
    return lax.dot_general(a, b, (((0,), (0,)), ((), ())), preferred_element_type=F32)


def rows_of(values, j):
    return jnp.broadcast_to(values[j : j + 1], (PACK, values.shape[1])).astype(BF)


class Peers:
    def __init__(self, layers, sectors):
        self.n = {"layer": layers, "phi": sectors}
        self.me = {"layer": lax.axis_index("layer"), "phi": lax.axis_index("phi")}

    def at(self, axis, distance):
        n = self.n[axis]
        there = lax.rem(self.me[axis] + (distance + n) % n, n)
        if axis == "layer":
            return (there, self.me["phi"])
        return (self.me["layer"], there)


def send(src, dst, send_sem, recv_sem, device):
    copy = pltpu.make_async_remote_copy(
        src_ref=src,
        dst_ref=dst,
        send_sem=send_sem,
        recv_sem=recv_sem,
        device_id=device,
        device_id_type=pl.DeviceIdType.MESH,
    )
    copy.start()
    return copy


class AllReduce:
    def __init__(self, peers, refs):
        self.peers = peers
        self.mine, self.got, self.part, self.full, self.sems = refs
        self.copies = []

    def _send(self, src, dst, k, device):
        copy = send(src, dst, self.sems.at[0, k], self.sems.at[1, k], device)
        self.copies.append(copy)
        return copy

    def start(self, values):
        sectors = self.peers.n["phi"]
        rows = self.mine.shape[1]
        for p in range(sectors):
            self.mine[p] = values[p * rows : (p + 1) * rows]
        me = self.peers.me["phi"]
        self.now = [
            self._send(
                self.mine.at[lax.rem(me + d, sectors)],
                self.got.at[d - 1],
                d - 1,
                self.peers.at("phi", d),
            )
            for d in range(1, sectors)
        ]

    def exchange(self):
        sectors, layers = self.peers.n["phi"], self.peers.n["layer"]
        for copy in self.now:
            copy.wait_recv()
        total = self.mine[self.peers.me["phi"]]
        for d in range(sectors - 1):
            total = total + self.got[d]
        me = self.peers.me["layer"]
        self.part[me] = total
        self.now = [
            self._send(
                self.part.at[me],
                self.part.at[me],
                sectors - 1 + d - 1,
                self.peers.at("layer", d),
            )
            for d in range(1, layers)
        ]

    def gather(self):
        sectors, layers = self.peers.n["phi"], self.peers.n["layer"]
        for copy in self.now:
            copy.wait_recv()
        total = self.part[0]
        for k in range(1, layers):
            total = total + self.part[k]
        me = self.peers.me["phi"]
        self.full[me] = total
        self.now = [
            self._send(
                self.full.at[me],
                self.full.at[me],
                sectors + layers - 2 + d - 1,
                self.peers.at("phi", d),
            )
            for d in range(1, sectors)
        ]

    def finish(self):
        for copy in self.now:
            copy.wait_recv()
        for copy in self.copies:
            copy.wait_send()


def kernel(
    layers,
    sectors,
    chunk,
    hits,
    index,
    weight,
    count,
    source,
    cot,
    w_message,
    w_edge,
    w_output,
    d_hits,
    g_message,
    g_edge,
    g_output,
    tile,
    message,
    message_t,
    iota,
    rim_out,
    rim_in,
    rim_sems,
    pool_out,
    pool_in,
    pool_sems,
    back_out,
    back_in,
    back_sems,
    early_mine,
    early_got,
    early_part,
    early_full,
    early_sems,
    late_mine,
    late_got,
    late_part,
    late_full,
    late_sems,
):
    peers = Peers(layers, sectors)
    me_l = peers.me["layer"]
    hit_rows = hits.shape[0]
    width = hits.shape[1]
    nodes = cot.shape[0]
    rim = nodes // 2
    share = nodes // layers
    groups = share // PACK
    chunks = hit_rows // chunk

    barrier = pltpu.get_barrier_semaphore()
    for axis in ("layer", "phi"):
        for d in range(1, peers.n[axis]):
            pl.semaphore_signal(
                barrier,
                inc=1,
                device_id=peers.at(axis, d),
                device_id_type=pl.DeviceIdType.MESH,
            )

    iota[...] = (
        (
            lax.broadcasted_iota(jnp.int32, (groups, PACK, LANES), 0) * PACK
            + lax.broadcasted_iota(jnp.int32, (groups, PACK, LANES), 1)
        )
        .astype(F32)
        .astype(BF)
    )

    upper = me_l // (layers // 2)

    def spread_share(base):
        parts = []
        for c in range(nodes // LANES):
            rows = (source[:, c * LANES : (c + 1) * LANES] - base).astype(F32)
            total = None
            for j in range(source.shape[0]):
                hit = jnp.where(iota[...] == rows_of(rows, j)[None], BF(1), BF(0))
                total = hit if total is None else total + hit
            parts.append(total.reshape(share, LANES))
        return dot(jnp.concatenate(parts, axis=1), cot[...])

    rim_out[...] = spread_share(
        me_l * share + (1 - upper) * (nodes + rim) - upper * rim
    ).astype(BF)

    pl.semaphore_wait(barrier, layers - 1 + sectors - 1)

    target = lax.rem(peers.me["phi"] + sectors + 1 - 2 * upper, sectors)
    rim_copy = send(rim_out, rim_in, rim_sems.at[0], rim_sems.at[1], (me_l, target))
    own_spread = spread_share(me_l * share + rim)

    def message_step(k, carry):
        at = pl.ds(pl.multiple_of(k * chunk, chunk), chunk)
        msg = jnp.tanh(dot(hits[at, :], w_message[...])).astype(BF)
        message[at, :width] = msg
        message[at, width:] = jnp.ones((chunk, LANES), BF)
        message_t[:, at] = msg.T
        return carry

    lax.fori_loop(0, chunks, message_step, 0)

    real_count = count[0, 0]

    def pool_share(e):
        base = lax.rem(me_l + e, layers) * share

        def step(k, acc):
            start = pl.multiple_of(k * chunk, chunk)
            for c in range(chunk // LANES):
                at = pl.ds(pl.multiple_of(start + c * LANES, LANES), LANES)
                rows = (index[:, at] - base).astype(F32)
                position = start + c * LANES + lax.broadcasted_iota(jnp.int32, rows.shape, 1)
                wts = jnp.where(position < real_count, weight[:, at].astype(F32), 0.0)
                total = jnp.zeros((groups, PACK, LANES), BF)
                for j in range(index.shape[0]):
                    total = jnp.where(
                        iota[...] == rows_of(rows, j)[None],
                        jnp.broadcast_to(rows_of(wts, j)[None], total.shape),
                        total,
                    )
                tile[e, :, at] = total.reshape(share, LANES)
            at = pl.ds(start, chunk)
            return acc + dot(tile[e, :, at], message[at, :])

        return lax.fori_loop(0, chunks, step, jnp.zeros((share, width + LANES), F32))

    pool_copies = []
    for e in range(1, layers):
        pool_out[e - 1] = pool_share(e).astype(BF)
        pool_copies.append(
            send(
                pool_out.at[e - 1],
                pool_in.at[e - 1],
                pool_sems.at[0, e - 1],
                pool_sems.at[1, e - 1],
                peers.at("layer", e),
            )
        )
    total = pool_share(0)
    for e, copy in enumerate(pool_copies):
        copy.wait_recv()
        total = total + pool_in[e].astype(F32)

    scale = (1.0 / jnp.sqrt(1.0 + total[:, width:])).astype(BF).astype(F32)
    node = (total[:, :width] * scale).astype(BF)
    pre = dot(node, w_edge[...])
    sigma = jax.nn.sigmoid(pre)
    rim_copy.wait_recv()
    spread = (own_spread + rim_in[...].astype(F32)).astype(BF)
    d_edge = dot_nt(spread, w_output[...])
    d_pre = (d_edge * (sigma * (1.0 + pre * (1.0 - sigma)))).astype(BF)
    own_cot = cot[pl.ds(pl.multiple_of(me_l * share, share), share), :].astype(F32)
    d_node = ((own_cot + dot_nt(d_pre, w_edge[...])) * scale).astype(BF)
    back_out[...] = d_node.T
    back_copies = [
        send(
            back_out,
            back_in.at[d - 1],
            back_sems.at[0, d - 1],
            back_sems.at[1, d - 1],
            peers.at("layer", d),
        )
        for d in range(1, layers)
    ]
    early = AllReduce(peers, (early_mine, early_got, early_part, early_full, early_sems))
    edge_msg = (pre * sigma).astype(BF)
    early.start(jnp.concatenate([dot_tn(node, d_pre), dot_tn(edge_msg, spread)], axis=0))

    for copy in back_copies:
        copy.wait_recv()
    d_nodes = jnp.concatenate(
        [back_out[...]] + [back_in[layers - e - 1] for e in range(1, layers)], axis=1
    )

    def back_step(k, acc):
        at = pl.ds(pl.multiple_of(k * chunk, chunk), chunk)
        tiles = jnp.concatenate([tile[e, :, at] for e in range(layers)], axis=0)
        d_message = dot(d_nodes, tiles)
        msg = message_t[:, at].astype(F32)
        d_act = (d_message * (1.0 - msg * msg)).astype(BF)
        d_hits[at, :] = dot_nt(d_act.T, w_message[...]).astype(BF)
        return acc + dot(d_act, hits[at, :])

    cuts = [chunks * i // 4 for i in range(5)]
    stages = [early.exchange, early.gather, early.finish, lambda: None]
    acc = jnp.zeros((width, width), F32)
    for i, stage in enumerate(stages):
        acc = lax.fori_loop(cuts[i], cuts[i + 1], back_step, acc)
        stage()

    late = AllReduce(peers, (late_mine, late_got, late_part, late_full, late_sems))
    late.start(acc.T)
    rim_copy.wait_send()
    for copy in pool_copies + back_copies:
        copy.wait_send()
    node_norm = math.sqrt(sectors * nodes)
    half = early_full.shape[0] // 2
    rows = early_full.shape[1]
    for p in range(half):
        g_edge[p * rows : (p + 1) * rows] = early_full[p] / node_norm
        g_output[p * rows : (p + 1) * rows] = early_full[half + p] / node_norm
    late.exchange()
    late.gather()
    late.finish()
    hit_norm = math.sqrt(layers * sectors * hit_rows)
    rows = late_full.shape[1]
    for p in range(sectors):
        g_message[p * rows : (p + 1) * rows] = late_full[p] / hit_norm


def reduce_scratch(layers, sectors, rows):
    part = rows // sectors
    return [
        pltpu.VMEM((sectors, part, LANES), F32),
        pltpu.VMEM((sectors - 1, part, LANES), F32),
        pltpu.VMEM((layers, part, LANES), F32),
        pltpu.VMEM((sectors, part, LANES), F32),
        pltpu.SemaphoreType.DMA((2, 2 * (sectors - 1) + layers - 1)),
    ]


def shards(hits, index, weight, counts, source, cot, w_message, w_edge, w_output):
    layers, sectors = lax.axis_size("layer"), lax.axis_size("phi")
    hit_rows, width = hits.shape[2:]
    nodes = cot.shape[1]
    share = nodes // layers
    vmem = pl.BlockSpec(memory_space=pltpu.VMEM)
    out = pl.pallas_call(
        functools.partial(kernel, layers, sectors, min(1024, hit_rows)),
        out_shape=(
            jax.ShapeDtypeStruct((hit_rows, width), BF),
            jax.ShapeDtypeStruct((width, width), F32),
            jax.ShapeDtypeStruct((width, width), F32),
            jax.ShapeDtypeStruct((width, width), F32),
        ),
        in_specs=[vmem, vmem, vmem, pl.BlockSpec(memory_space=pltpu.SMEM)] + [vmem] * 5,
        out_specs=(vmem, vmem, vmem, vmem),
        scratch_shapes=[
            pltpu.VMEM((layers, share, hit_rows), BF),
            pltpu.VMEM((hit_rows, width + LANES), BF),
            pltpu.VMEM((width, hit_rows), BF),
            pltpu.VMEM((share // PACK, PACK, LANES), BF),
            pltpu.VMEM((share, width), BF),
            pltpu.VMEM((share, width), BF),
            pltpu.SemaphoreType.DMA((2,)),
            pltpu.VMEM((layers - 1, share, width + LANES), BF),
            pltpu.VMEM((layers - 1, share, width + LANES), BF),
            pltpu.SemaphoreType.DMA((2, layers - 1)),
            pltpu.VMEM((width, share), BF),
            pltpu.VMEM((layers - 1, width, share), BF),
            pltpu.SemaphoreType.DMA((2, layers - 1)),
        ]
        + reduce_scratch(layers, sectors, 2 * width)
        + reduce_scratch(layers, sectors, width),
        compiler_params=pltpu.CompilerParams(
            collective_id=0, has_side_effects=True, vmem_limit_bytes=56 * 1024 * 1024
        ),
    )(
        hits[0, 0],
        index[0, 0],
        weight[0, 0],
        counts,
        source[0],
        cot[0],
        w_message,
        w_edge,
        w_output,
    )
    return (out[0][None, None],) + tuple(out[1:])


def solution(mesh):
    placed = (
        P("layer", "phi", None, None),
        P("layer", "phi", None, None),
        P("layer", "phi", None, None),
        P("layer", "phi"),
        P("phi", None, None),
        P("phi", None, None),
        P(),
        P(),
        P(),
    )
    return jax.shard_map(
        shards,
        mesh=mesh,
        in_specs=placed,
        out_specs=(P("layer", "phi", None, None), P(), P(), P()),
        check_vma=False,
    )
```

time: 370 us -> 76.4 us (0.21)
  waiting for transfers between devices: 153 us -> 0 us
  matrix products: 112 us -> 0 us
  Pallas kernels: 0 us -> 69.9 us
  other arithmetic: 37.5 us -> 0 us
  local copies, waits for them, and re-layouts: 31.6 us -> 4.99 us
  between operations: 14.8 us -> 1.31 us
  blocking collectives: 10 us -> 0 us
  starting transfers between devices: 7.16 us -> 0 us
    psum x2 -> x0, waiting for transfers between devices: 153 us -> none  [the longest x1 121 us: shards(): summed = lax.psum((message_term, edge_term, output_term), ('layer', 'phi'))]
    dot_general x41 -> x0, matrix products: 112 us -> none  [the longest x20 51.8 us: contract_rows(): lax.dot_general(left, right, (((0,), (0,)), ((), ())), preferred_element_...]
    pallas_call x0 -> x1, Pallas kernels: none -> 69.9 us  [shards(): pl.pallas_call(functools.partial(kernel, layers, sectors, min(1024, hit_r...]
    slice x65 -> x0, local copies, waits for them, and re-layouts: 29.8 us -> none  [the longest x32 27.4 us: one_hot_tile(): index_blk[0][None, :]]
    reduce_sum x17 -> x0, other arithmetic: 29.4 us -> none  [the longest x1 14.9 us: shards(): jnp.sum((ext_iota == sources[:, None, :]).astype(jnp.float32), axis=0)]
    psum x1 -> x0, blocking collectives: 10 us -> none  [shards(): totals, mass_sum = lax.psum((pooled, masses), 'layer')]
    ppermute x4 -> x0, starting transfers between devices: 7.08 us -> none  [the longest x2 7.07 us: with_halo(): lax.ppermute(head, axis, [((i + 1) % count, i) for i in range(count)])]
    unnamed x15 -> x10, local copies, waits for them, and re-layouts: 0.77 us -> 4.99 us
  transfers between devices with their start and end apart: 6 -> 0, of which waited for: 2 -> 0; matrix products, arithmetic and copies ran while one was open for 41% -> 0% of each run, Pallas kernels for 0% -> 0%
where the time goes in v1:
time: 76.4 us; the launch traced here: 76.2 us
  Pallas kernels  69.9 us (91%)
  local copies, waits for them, and re-layouts  4.99 us (7%)
  between operations  1.31 us (2%)
    pallas_call x1, Pallas kernels, shards(): pl.pallas_call(functools.partial(kernel, layers, sectors, min(1024, hit_r...  69.9 us
    unnamed x10, local copies, waits for them, and re-layouts  4.99 us

profile of v1, /device:TPU:0, one launch (start us, length us, event | category | flops | bytes accessed | tf_op | source)
XLA Modules:
  0.0 76.2 jit_solution(2569176311885842525)
XLA Ops:
  1.3 69.9 %shard_map.120 = (bf16[8192,128]{1,0:T(8,128)(2,1)}, f32[128,128]{1,0:T(8,128)}, f32[128,128]{1,0:T(8,128)}, f32[128,128]{1,0:T(8,128)}) custom-call(bf16[8192,128]{1,0:T(8,128)(2,1)} %bitcast.6, s32[4,8192]{1,0:T(4,128)} %bitcast.9, bf16[4,8192]{1,0:T(4,128)(2,1)} %bitcast.10, s32[1,1]{1,0:T(1,128)S(6)} %copy.17.count, s32[8,1024]{1,0:T(8,128)} %bitcast.11, ...), custom_call_target="tpu_custom_call" | custom-call | tf_op jit(solution)/shard_map/pallas_call | solution.py:360
  71.2 0.0 copy-start.2
  71.2 0.0 copy-start.1
  71.2 0.0 copy-start
  71.2 3.1 %copy.18 = bf16[1,1,8192,128]{3,2,1,0:T(8,128)(2,1)} copy(bf16[1,1,8192,128]{3,2,1,0:T(8,128)(2,1)} %bitcast.7) | data formatting | bytes 4194304
  74.3 0.0 copy-done.2
  74.3 0.6 copy.19
  75.0 0.0 copy-done.1
  75.0 0.6 copy.20
  75.6 0.0 copy-done
  75.6 0.6 copy.21
Async XLA Ops:
  71.2 3.1 %copy-start.2 = (f32[128,128]{1,0:T(8,128)S(1)}, f32[128,128]{1,0:T(8,128)}, u32[]{:S(2)}) copy-start(f32[128,128]{1,0:T(8,128)} %get-tuple-element.17) | copy-start | bytes 196612
  71.2 3.7 %copy-start.1 = (f32[128,128]{1,0:T(8,128)S(1)}, f32[128,128]{1,0:T(8,128)}, u32[]{:S(2)}) copy-start(f32[128,128]{1,0:T(8,128)} %get-tuple-element.18) | copy-start | bytes 196612
  71.2 4.4 %copy-start = (f32[128,128]{1,0:T(8,128)S(1)}, f32[128,128]{1,0:T(8,128)}, u32[]{:S(2)}) copy-start(f32[128,128]{1,0:T(8,128)} %get-tuple-element.19) | copy-start | bytes 196612

commit v2 on v1

--- a/solution.py
+++ b/solution.py
@@ -26,8 +26,8 @@
     return lax.dot_general(a, b, (((0,), (0,)), ((), ())), preferred_element_type=F32)
 
 
-def rows_of(values, j):
-    return jnp.broadcast_to(values[j : j + 1], (PACK, values.shape[1])).astype(BF)
+def rows_of(values, j, dtype):
+    return jnp.broadcast_to(values[j : j + 1], (PACK, values.shape[1])).astype(dtype)
 
 
 class Peers:
@@ -37,14 +37,14 @@
 
     def at(self, axis, distance):
         n = self.n[axis]
-        there = lax.rem(self.me[axis] + (distance + n) % n, n)
+        there = lax.rem(self.me[axis] + distance, n)
         if axis == "layer":
             return (there, self.me["phi"])
         return (self.me["layer"], there)
 
 
-def send(src, dst, send_sem, recv_sem, device):
-    copy = pltpu.make_async_remote_copy(
+def remote(src, dst, send_sem, recv_sem, device):
+    return pltpu.make_async_remote_copy(
         src_ref=src,
         dst_ref=dst,
         send_sem=send_sem,
@@ -52,6 +52,10 @@
         device_id=device,
         device_id_type=pl.DeviceIdType.MESH,
     )
+
+
+def send(*what):
+    copy = remote(*what)
     copy.start()
     return copy
 
@@ -145,7 +149,11 @@
     g_message,
     g_edge,
     g_output,
-    tile,
+    tile_a,
+    tile_b,
+    pooled,
+    node_rows,
+    weight_rows,
     message,
     message_t,
     iota,
@@ -194,8 +202,7 @@
             lax.broadcasted_iota(jnp.int32, (groups, PACK, LANES), 0) * PACK
             + lax.broadcasted_iota(jnp.int32, (groups, PACK, LANES), 1)
         )
-        .astype(F32)
-        .astype(BF)
+        .astype(jnp.int16)
     )
 
     upper = me_l // (layers // 2)
@@ -203,10 +210,10 @@
     def spread_share(base):
         parts = []
         for c in range(nodes // LANES):
-            rows = (source[:, c * LANES : (c + 1) * LANES] - base).astype(F32)
+            rows = source[:, c * LANES : (c + 1) * LANES] - base
             total = None
             for j in range(source.shape[0]):
-                hit = jnp.where(iota[...] == rows_of(rows, j)[None], BF(1), BF(0))
+                hit = jnp.where(iota[...] == rows_of(rows, j, jnp.int16)[None], BF(1), BF(0))
                 total = hit if total is None else total + hit
             parts.append(total.reshape(share, LANES))
         return dot(jnp.concatenate(parts, axis=1), cot[...])
@@ -215,11 +222,11 @@
         me_l * share + (1 - upper) * (nodes + rim) - upper * rim
     ).astype(BF)
 
-    pl.semaphore_wait(barrier, layers - 1 + sectors - 1)
-
     target = lax.rem(peers.me["phi"] + sectors + 1 - 2 * upper, sectors)
-    rim_copy = send(rim_out, rim_in, rim_sems.at[0], rim_sems.at[1], (me_l, target))
+    rim_copy = remote(rim_out, rim_in, rim_sems.at[0], rim_sems.at[1], (me_l, target))
     own_spread = spread_share(me_l * share + rim)
+
+    real_count = count[0, 0]
 
     def message_step(k, carry):
         at = pl.ds(pl.multiple_of(k * chunk, chunk), chunk)
@@ -227,48 +234,80 @@
         message[at, :width] = msg
         message[at, width:] = jnp.ones((chunk, LANES), BF)
         message_t[:, at] = msg.T
+        position = k * chunk + lax.broadcasted_iota(jnp.int32, (4, chunk), 1)
+        weights = jnp.where(position < real_count, weight[:, at].astype(F32), 0.0)
+        nodes_of = index[:, at]
+        for j in range(4):
+            node_rows[j, :, at] = rows_of(nodes_of, j, jnp.int16)
+            weight_rows[j, :, at] = rows_of(weights, j, BF)
         return carry
 
     lax.fori_loop(0, chunks, message_step, 0)
 
-    real_count = count[0, 0]
-
-    def pool_share(e):
-        base = lax.rem(me_l + e, layers) * share
-
-        def step(k, acc):
-            start = pl.multiple_of(k * chunk, chunk)
-            for c in range(chunk // LANES):
-                at = pl.ds(pl.multiple_of(start + c * LANES, LANES), LANES)
-                rows = (index[:, at] - base).astype(F32)
-                position = start + c * LANES + lax.broadcasted_iota(jnp.int32, rows.shape, 1)
-                wts = jnp.where(position < real_count, weight[:, at].astype(F32), 0.0)
-                total = jnp.zeros((groups, PACK, LANES), BF)
-                for j in range(index.shape[0]):
-                    total = jnp.where(
-                        iota[...] == rows_of(rows, j)[None],
-                        jnp.broadcast_to(rows_of(wts, j)[None], total.shape),
-                        total,
-                    )
-                tile[e, :, at] = total.reshape(share, LANES)
-            at = pl.ds(start, chunk)
-            return acc + dot(tile[e, :, at], message[at, :])
-
-        return lax.fori_loop(0, chunks, step, jnp.zeros((share, width + LANES), F32))
-
-    pool_copies = []
-    for e in range(1, layers):
-        pool_out[e - 1] = pool_share(e).astype(BF)
-        pool_copies.append(
-            send(
-                pool_out.at[e - 1],
-                pool_in.at[e - 1],
-                pool_sems.at[0, e - 1],
-                pool_sems.at[1, e - 1],
-                peers.at("layer", e),
-            )
+    pairs = chunks // 2
+    slots = index.shape[0]
+
+    def build(tile, e, i, k):
+        base = (lax.rem(me_l + e, layers) * share).astype(jnp.int16)
+        for c in range(chunk // LANES):
+            at = pl.ds(pl.multiple_of(k * chunk + c * LANES, LANES), LANES)
+            total = jnp.zeros((groups, PACK, LANES), BF)
+            for j in range(slots):
+                total = jnp.where(
+                    iota[...] == (node_rows[j, :, at] - base)[None],
+                    jnp.broadcast_to(weight_rows[j, :, at][None], total.shape),
+                    total,
+                )
+            to = pl.ds(pl.multiple_of(i * chunk + c * LANES, LANES), LANES)
+            tile[e, :, to] = total.reshape(share, LANES)
+
+    def use(tile, e, i, k):
+        of = pl.ds(pl.multiple_of(i * chunk, chunk), chunk)
+        at = pl.ds(pl.multiple_of(k * chunk, chunk), chunk)
+        pooled[...] += dot(tile[e, :, of], message[at, :])
+
+    def pool_copy(e):
+        return remote(
+            pool_out.at[e - 1],
+            pool_in.at[e - 1],
+            pool_sems.at[0, e - 1],
+            pool_sems.at[1, e - 1],
+            peers.at("layer", e),
         )
-    total = pool_share(0)
+
+    build(tile_a, 1, 0, 0)
+
+    def pool_share(step, carry):
+        e = lax.rem(step, layers)
+        pooled[...] = jnp.zeros_like(pooled)
+
+        def pair(i, carry):
+            after = i + 1
+            wrap = after // pairs
+            after = after - wrap * pairs
+            build(tile_b, e, i, 2 * i + 1)
+            use(tile_a, e, i, 2 * i)
+            build(tile_a, lax.rem(step + wrap, layers), after, 2 * after)
+            use(tile_b, e, i, 2 * i + 1)
+            return carry
+
+        lax.fori_loop(0, pairs, pair, 0)
+
+        @pl.when(step == 1)
+        def _():
+            pl.semaphore_wait(barrier, layers - 1 + sectors - 1)
+            rim_copy.start()
+
+        @pl.when(step < layers)
+        def _():
+            pool_out[step - 1] = pooled[...].astype(BF)
+            pool_copy(step).start()
+
+        return carry
+
+    lax.fori_loop(1, layers + 1, pool_share, 0)
+    pool_copies = [pool_copy(e) for e in range(1, layers)]
+    total = pooled[...]
     for e, copy in enumerate(pool_copies):
         copy.wait_recv()
         total = total + pool_in[e].astype(F32)
@@ -304,24 +343,38 @@
         [back_out[...]] + [back_in[layers - e - 1] for e in range(1, layers)], axis=1
     )
 
-    def back_step(k, acc):
+    def back_step(tile, i, k, acc):
+        of = pl.ds(pl.multiple_of(i * chunk, chunk), chunk)
         at = pl.ds(pl.multiple_of(k * chunk, chunk), chunk)
-        tiles = jnp.concatenate([tile[e, :, at] for e in range(layers)], axis=0)
+        tiles = jnp.concatenate([tile[e, :, of] for e in range(layers)], axis=0)
         d_message = dot(d_nodes, tiles)
         msg = message_t[:, at].astype(F32)
         d_act = (d_message * (1.0 - msg * msg)).astype(BF)
-        d_hits[at, :] = dot_nt(d_act.T, w_message[...]).astype(BF)
+        message_t[:, at] = d_act
         return acc + dot(d_act, hits[at, :])
 
-    cuts = [chunks * i // 4 for i in range(5)]
-    stages = [early.exchange, early.gather, early.finish, lambda: None]
-    acc = jnp.zeros((width, width), F32)
-    for i, stage in enumerate(stages):
-        acc = lax.fori_loop(cuts[i], cuts[i + 1], back_step, acc)
-        stage()
-
+    def back_pair(i, acc):
+        acc = back_step(tile_a, i, 2 * i, acc)
+        return back_step(tile_b, i, 2 * i + 1, acc)
+
+    acc = lax.fori_loop(0, pairs, back_pair, jnp.zeros((width, width), F32))
     late = AllReduce(peers, (late_mine, late_got, late_part, late_full, late_sems))
     late.start(acc.T)
+    early.exchange()
+
+    def hit_step(k, carry):
+        at = pl.ds(pl.multiple_of(k * chunk, chunk), chunk)
+        d_hits[at, :] = dot_nt(message_t[:, at].T, w_message[...]).astype(BF)
+        return carry
+
+    cuts = [chunks * i // 3 for i in range(4)]
+    lax.fori_loop(cuts[0], cuts[1], hit_step, 0)
+    late.exchange()
+    early.gather()
+    lax.fori_loop(cuts[1], cuts[2], hit_step, 0)
+    late.gather()
+    early.finish()
+    lax.fori_loop(cuts[2], cuts[3], hit_step, 0)
     rim_copy.wait_send()
     for copy in pool_copies + back_copies:
         copy.wait_send()
@@ -331,8 +384,6 @@
     for p in range(half):
         g_edge[p * rows : (p + 1) * rows] = early_full[p] / node_norm
         g_output[p * rows : (p + 1) * rows] = early_full[half + p] / node_norm
-    late.exchange()
-    late.gather()
     late.finish()
     hit_norm = math.sqrt(layers * sectors * hit_rows)
     rows = late_full.shape[1]
@@ -358,7 +409,7 @@
     share = nodes // layers
     vmem = pl.BlockSpec(memory_space=pltpu.VMEM)
     out = pl.pallas_call(
-        functools.partial(kernel, layers, sectors, min(1024, hit_rows)),
+        functools.partial(kernel, layers, sectors, min(2048, hit_rows // 2)),
         out_shape=(
             jax.ShapeDtypeStruct((hit_rows, width), BF),
             jax.ShapeDtypeStruct((width, width), F32),
@@ -368,10 +419,14 @@
         in_specs=[vmem, vmem, vmem, pl.BlockSpec(memory_space=pltpu.SMEM)] + [vmem] * 5,
         out_specs=(vmem, vmem, vmem, vmem),
         scratch_shapes=[
-            pltpu.VMEM((layers, share, hit_rows), BF),
+            pltpu.VMEM((layers, share, hit_rows // 2), BF),
+            pltpu.VMEM((layers, share, hit_rows // 2), BF),
+            pltpu.VMEM((share, width + LANES), F32),
+            pltpu.VMEM((4, PACK, hit_rows), jnp.int16),
+            pltpu.VMEM((4, PACK, hit_rows), BF),
             pltpu.VMEM((hit_rows, width + LANES), BF),
             pltpu.VMEM((width, hit_rows), BF),
-            pltpu.VMEM((share // PACK, PACK, LANES), BF),
+            pltpu.VMEM((share // PACK, PACK, LANES), jnp.int16),
             pltpu.VMEM((share, width), BF),
             pltpu.VMEM((share, width), BF),
             pltpu.SemaphoreType.DMA((2,)),

time: 76.4 us -> 64 us (0.84)
  Pallas kernels: 69.9 us -> 57.5 us
    pallas_call x1, Pallas kernels: 69.9 us -> 57.5 us  [shards(): pl.pallas_call(functools.partial(kernel, layers, sectors, min(2048, hit_r...]
where the time goes in v2:
time: 64 us; the launch traced here: 63.8 us
  Pallas kernels  57.5 us (90%)
  local copies, waits for them, and re-layouts  4.99 us (8%)
  between operations  1.31 us (2%)
    pallas_call x1, Pallas kernels, shards(): pl.pallas_call(functools.partial(kernel, layers, sectors, min(2048, hit_r...  57.5 us
    unnamed x10, local copies, waits for them, and re-layouts  4.99 us

profile of v2, /device:TPU:0, one launch (start us, length us, event | category | flops | bytes accessed | tf_op | source)
XLA Modules:
  0.0 63.8 jit_solution(3823008681593430622)
XLA Ops:
  1.3 57.5 %shard_map.120 = (bf16[8192,128]{1,0:T(8,128)(2,1)}, f32[128,128]{1,0:T(8,128)}, f32[128,128]{1,0:T(8,128)}, f32[128,128]{1,0:T(8,128)}) custom-call(bf16[8192,128]{1,0:T(8,128)(2,1)} %bitcast.6, s32[4,8192]{1,0:T(4,128)} %bitcast.9, bf16[4,8192]{1,0:T(4,128)(2,1)} %bitcast.10, s32[1,1]{1,0:T(1,128)S(6)} %copy.17.count, s32[8,1024]{1,0:T(8,128)} %bitcast.11, ...), custom_call_target="tpu_custom_call" | custom-call | tf_op jit(solution)/shard_map/pallas_call | solution.py:411
  58.8 0.0 copy-start.2
  58.8 0.0 copy-start.1
  58.8 0.0 copy-start
  58.8 3.1 %copy.18 = bf16[1,1,8192,128]{3,2,1,0:T(8,128)(2,1)} copy(bf16[1,1,8192,128]{3,2,1,0:T(8,128)(2,1)} %bitcast.7) | data formatting | bytes 4194304
  61.9 0.0 copy-done.2
  61.9 0.6 copy.19
  62.6 0.0 copy-done.1
  62.6 0.6 copy.20
  63.2 0.0 copy-done
  63.2 0.6 copy.21
Async XLA Ops:
  58.8 3.1 %copy-start.2 = (f32[128,128]{1,0:T(8,128)S(1)}, f32[128,128]{1,0:T(8,128)}, u32[]{:S(2)}) copy-start(f32[128,128]{1,0:T(8,128)} %get-tuple-element.17) | copy-start | bytes 196612
  58.8 3.7 %copy-start.1 = (f32[128,128]{1,0:T(8,128)S(1)}, f32[128,128]{1,0:T(8,128)}, u32[]{:S(2)}) copy-start(f32[128,128]{1,0:T(8,128)} %get-tuple-element.18) | copy-start | bytes 196612
  58.8 4.4 %copy-start = (f32[128,128]{1,0:T(8,128)S(1)}, f32[128,128]{1,0:T(8,128)}, u32[]{:S(2)}) copy-start(f32[128,128]{1,0:T(8,128)} %get-tuple-element.19) | copy-start | bytes 196612
